TPU v7x, 1024 devices: a whole 8x8x8 slice. The times are simulated.
1024 devices in a mesh: dp: 128 (over x, z, core), fsdp: 8 (over y).
Axes of the slice: x: 8, y: 8, z: 8, core: 2. Of those that a mesh axis runs over, the one named last changes fastest.
Arguments:
- frames: bfloat16 [262144, 1024], P(('dp', 'fsdp')), may hold values from -6 to 6
- lengths: int32 [1024], replicated, may hold values from 1 to 768, 262144 in all
- taps: bfloat16 [31, 1024], P(None, 'fsdp'), may hold values from -1.8 to 1.8
- conv_bias: bfloat16 [1024], P('fsdp'), may hold values from -3 to 3
- norm_gain: bfloat16 [1024], P('fsdp'), may hold values from 0.5 to 2
- proj_weight: bfloat16 [1024, 1024], P(None, 'fsdp'), may hold values from -0.1875 to 0.1875
- cotangent: bfloat16 [262144, 1024], P(('dp', 'fsdp')), may hold values from -6 to 6
Outputs:
- outputs: bfloat16 [262144, 1024], P(('dp', 'fsdp'))
- frame_grad: bfloat16 [262144, 1024], P(('dp', 'fsdp'))
- proj_grad: float32 [1024, 1024], P('dp', 'fsdp')
Inputs may be any that keep to these rules, and one draw needn't show every extreme that they name: The lengths sum to 262144; the longest recording has exactly 768 frames.
All inputs are finite; a program needn't handle non-finite values.
Results may differ from a plain program's by a relative error of at most 0.0049.
Values may be sent and summed in bfloat16 or wider, within the bound.
A program may use at most 32 MiB of HBM per device.

v0:
```python
import jax
import jax.numpy as jnp
from jax import lax
from jax.sharding import PartitionSpec as P


def extended(value, sides, width):
    for axis, dim in sides:
        devices, length = (lax.axis_size(axis), value.shape[dim])
        up = [(i, (i + 1) % devices) for i in range(devices - 1)]
        down = [(j, i) for i, j in up]
        last = lax.slice_in_dim(value, length - width, length, axis=dim)
        first = lax.slice_in_dim(value, 0, width, axis=dim)
        before = lax.ppermute(last, axis, up)
        after = lax.ppermute(first, axis, down)
        value = jnp.concatenate([before, value, after], axis=dim)
    return value


def locate(global_rows, lengths):
    ends = jnp.cumsum(lengths)
    starts = ends - lengths
    record = jnp.sum((ends[None, :] <= global_rows[:, None]).astype(jnp.int32), axis=1)
    chosen = jnp.arange(lengths.shape[0], dtype=jnp.int32)[None, :] == record[:, None]
    start = jnp.sum(jnp.where(chosen, starts[None, :], 0), axis=1)
    span = jnp.sum(jnp.where(chosen, lengths[None, :], 0), axis=1)
    return (global_rows - start, span)


def depthwise(window, taps, bias, offsets, span):
    margin = (taps.shape[0] - 1) // 2
    row_count = window.shape[0] - 2 * margin
    result = jnp.zeros((row_count, window.shape[1]), jnp.float32) + bias
    for tap in range(taps.shape[0]):
        moved = offsets + (tap - margin)
        valid = ((moved >= 0) & (moved < span)).astype(jnp.float32)[:, None]
        result = result + taps[tap] * window[tap : tap + row_count] * valid
    return result


def depthwise_back(grads, taps, offsets, span):
    margin = (taps.shape[0] - 1) // 2
    row_count = grads.shape[0] - 2 * margin
    result = jnp.zeros((row_count, grads.shape[1]), jnp.float32)
    for tap in range(taps.shape[0]):
        start = 2 * margin - tap
        moved = offsets + (margin - tap)
        valid = ((moved >= 0) & (moved < span)).astype(jnp.float32)[:, None]
        result = result + taps[tap] * grads[start : start + row_count] * valid
    return result


def forward(window, offsets, span, taps_float, bias_float, gain_float):
    conv_out = depthwise(window.astype(jnp.float32), taps_float, bias_float, offsets, span)
    centre = conv_out - jnp.mean(conv_out, axis=-1, keepdims=True)
    inverse = lax.rsqrt(jnp.mean(centre * centre, axis=-1, keepdims=True) + 1e-05)
    normed = centre * inverse
    scaled = normed * gain_float
    sigmoid_gate = jax.nn.sigmoid(scaled)
    swished = (scaled * sigmoid_gate).astype(jnp.bfloat16)
    return (normed, inverse, scaled, sigmoid_gate, swished)


def backward(grad_out, state, weight, gain_float):
    normed, inverse, scaled, sigmoid_gate, swished = state
    grad_swish = lax.dot_general(
        grad_out, weight, (((1,), (1,)), ((), ())), preferred_element_type=jnp.float32
    )
    grad_scaled = grad_swish * (sigmoid_gate + scaled * sigmoid_gate * (1.0 - sigmoid_gate))
    grad_normed = grad_scaled * gain_float
    return inverse * (
        grad_normed
        - jnp.mean(grad_normed, axis=-1, keepdims=True)
        - normed * jnp.mean(grad_normed * normed, axis=-1, keepdims=True)
    )


def per_device(frames, lengths, taps, conv_bias, norm_gain, proj_weight, cotangent):
    weight, taps_all, bias_all, gain_all = (
        lax.all_gather(proj_weight, "fsdp", axis=1, tiled=True),
        lax.all_gather(taps, "fsdp", axis=1, tiled=True),
        lax.all_gather(conv_bias, "fsdp", axis=0, tiled=True),
        lax.all_gather(norm_gain, "fsdp", axis=0, tiled=True),
    )
    row_count = frames.shape[0]
    margin = (taps_all.shape[0] - 1) // 2
    device = lax.axis_index("dp") * lax.axis_size("fsdp") + lax.axis_index("fsdp")
    first_row = device * row_count
    taps_float = taps_all.astype(jnp.float32)
    bias_float = bias_all.astype(jnp.float32)
    gain_float = gain_all.astype(jnp.float32)
    window = extended(frames, ((("dp", "fsdp"), 0),), margin)
    offsets, span = locate(first_row + jnp.arange(row_count, dtype=jnp.int32), lengths)
    state = forward(window, offsets, span, taps_float, bias_float, gain_float)
    swished_mid = state[4]
    grad_conv = backward(cotangent, state, weight, gain_float)
    grad_window = extended(grad_conv, ((("dp", "fsdp"), 0),), margin)
    outputs = jnp.dot(swished_mid, weight, preferred_element_type=jnp.float32).astype(jnp.bfloat16)
    grad_values = depthwise_back(grad_window, taps_float, offsets, span)
    frame_grad = grad_values.astype(jnp.bfloat16)
    weight_term = lax.dot_general(
        swished_mid, cotangent, (((0,), (0,)), ((), ())), preferred_element_type=jnp.float32
    )
    group_sum = lax.psum_scatter(weight_term, "fsdp", scatter_dimension=1, tiled=True)
    summed = lax.psum_scatter(group_sum, "dp", scatter_dimension=0, tiled=True)
    proj_grad = summed * (1.0 / lengths.shape[0])
    return (outputs, frame_grad, proj_grad)


def solution(mesh):
    in_specs = (
        P(("dp", "fsdp"), None),
        P(),
        P(None, "fsdp"),
        P("fsdp"),
        P("fsdp"),
        P(None, "fsdp"),
        P(("dp", "fsdp"), None),
    )
    out_specs = (P(("dp", "fsdp"), None), P(("dp", "fsdp"), None), P("dp", "fsdp"))
    return jax.shard_map(
        per_device, mesh=mesh, in_specs=in_specs, out_specs=out_specs, check_vma=False
    )
```

profile of v0, /device:TPU:1, one launch (start us, length us, event | category | flops | bytes accessed | tf_op | source)
XLA Modules:
  0.0 366.6 jit_solution(11217438940055339930)
XLA Ops:
  7.2 0.0 copy-start
  7.2 0.0 copy-start.1
  7.2 0.0 all-gather.4.cloned.1.call-start
  7.2 0.9 fusion.193
  8.1 4.1 %collective-permute-start = (bf16[15,1024]{1,0:T(8,128)(2,1)S(1)}, bf16[15,1024]{1,0:T(8,128)(2,1)S(1)}, u32[]{:S(2)}, u32[]{:S(2)}) collective-permute-start(bf16[15,1024]{1,0:T(8,128)(2,1)S(1)} %get-tuple-element.15), channel_id=1, source_target_pairs={{0,1},{1,2},{2,3},{3,4},{4,5},{5,6},{6,7},{7,8},{8,9},{9,10},{10,1... | collective-permute-start | bytes 92168 | tf_op jit(solution)/shard_map/ppermute | solution.py:14
  12.3 5.1 %collective-permute-start.1 = (bf16[15,1024]{1,0:T(8,128)(2,1)S(1)}, bf16[15,1024]{1,0:T(8,128)(2,1)S(1)}, u32[]{:S(2)}, u32[]{:S(2)}) collective-permute-start(bf16[15,1024]{1,0:T(8,128)(2,1)S(1)} %get-tuple-element.16), channel_id=1, source_target_pairs={{1,0},{2,1},{3,2},{4,3},{5,4},{6,5},{7,6},{8,7},{9,8},{10,9},{11,1... | collective-permute-start | bytes 92168 | tf_op jit(solution)/shard_map/ppermute | solution.py:15
  17.3 0.0 all-gather.4.cloned.1.call-update
  17.4 0.0 reduce-scatter.2.cloned.1.call-start
  17.4 1.0 reduce-window.9
  18.4 0.1 slice.360
  18.5 0.1 slice_reduce_fusion
  18.6 0.8 fusion.191
  19.4 0.2 convert_reduce_fusion
  19.6 1.1 select_reduce_fusion.1
  20.7 17.1 %all_gather.13 = bf16[31,1024]{1,0:T(8,128)(2,1)S(1)} all-gather(bf16[31,128]{1,0:T(8,128)(2,1)} %param.9), channel_id=1, replica_groups=mesh['dp'=128,'fsdp'=8] {'fsdp'}, dimensions={1}, use_global_device_ids=true | all-gather | bytes 71424 | tf_op jit(solution)/shard_map/all_gather | solution.py:81
  37.9 0.1 fusion.194
  38.0 10.3 %all-gather = bf16[8,1,128]{2,1,0:T(2,128)(2,1)S(1)} all-gather(bf16[1,1,128]{2,1,0:T(2,128)(2,1)} %bitcast.111), channel_id=1, replica_groups=mesh['dp'=128,'fsdp'=8] {'fsdp'}, dimensions={0}, use_global_device_ids=true | all-gather | bytes 2304 | tf_op jit(solution)/shard_map/all_gather | solution.py:82
  48.4 12.0 %all-gather.1 = bf16[8,1,128]{2,1,0:T(2,128)(2,1)S(1)} all-gather(bf16[1,1,128]{2,1,0:T(2,128)(2,1)} %bitcast.112), channel_id=1, replica_groups=mesh['dp'=128,'fsdp'=8] {'fsdp'}, dimensions={0}, use_global_device_ids=true | all-gather | bytes 2304 | tf_op jit(solution)/shard_map/all_gather | solution.py:83
  60.4 0.0 collective-permute-done
  60.4 0.0 collective-permute-done.1
  60.4 0.0 copy-done.1
  60.4 0.2 maximum_convert_fusion
  60.6 6.3 %fusion.188 = (f32[256]{0:T(256)S(1)}, f32[256,1024]{1,0:T(8,128)S(1)}) fusion(f32[256]{0:T(256)S(1)} %get-tuple-element.49, f32[286,1024]{1,0:T(8,128)S(1)} %maximum_convert_fusion, f32[1024]{0:T(1024)S(1)} %bitcast.66, f32[256]{0:T(256)S(1)} %get-tuple-element.50, f32[1024]{0:T(1024)S(1)} %bitcast.64, f32[256]{0:T(256)S(1)} %get-tuple-element.51, ...), kind=kLoop, calls=%fused_computation.323 | loop fusion | flops 24641280 | bytes 33718272 | tf_op jit(solution)/shard_map/reduce_sum | solution.py:55
  66.9 0.2 multiply_reduce_fusion.1
  67.1 0.0 copy-done
  67.1 2.9 fusion.184
  70.0 0.0 reduce-scatter.2.cloned.1.call-update
  70.1 0.0 all-reduce.3.cloned.1.call-start
  70.1 1.3 dynamic-slice
  72.0 4.3 %all-gather.4.cloned.1.call-done = bf16[1024,1024]{1,0:T(8,128)(2,1)} async-done(((bf16[1024,128]{1,0:T(8,128)(2,1)}), bf16[1024,1024]{1,0:T(8,128)(2,1)}) %all-gather.4.cloned.1.call-update) | async-done | bytes 2097168 | tf_op jit(solution)/shard_map/all_gather | solution.py:80
  76.3 2.8 fusion.187
  79.1 0.0 copy-start.2
  79.1 0.3 subtract_multiply_fusion
  79.5 18.1 %collective-permute-start.2 = (f32[15,1024]{1,0:T(8,128)S(1)}, f32[15,1024]{1,0:T(8,128)S(1)}, u32[]{:S(2)}, u32[]{:S(2)}) collective-permute-start(f32[15,1024]{1,0:T(8,128)S(1)} %get-tuple-element.13), channel_id=1, source_target_pairs={{1,0},{2,1},{3,2},{4,3},{5,4},{6,5},{7,6},{8,7},{9,8},{10,9},{11,1... | collective-permute-start | bytes 184328 | tf_op jit(solution)/shard_map/ppermute | solution.py:15
  97.6 1.9 collective-permute-start.3
  99.5 0.0 copy-done.2
  99.5 1.7 convolution_convert_fusion
  101.2 50.0 %reduce-scatter.2.cloned.1.call-done = f32[1024,128]{1,0:T(8,128)} async-done(((f32[1024,1024]{1,0:T(8,128)}), f32[1024,128]{1,0:T(8,128)}) %reduce-scatter.2.cloned.1.call-update) | async-done | bytes 524304 | tf_op jit(solution)/shard_map/reduce_scatter | solution.py:104
  151.2 0.0 all-reduce.3.cloned.1.call-update
  151.2 0.0 collective-permute-done.2
  151.2 0.0 collective-permute-done.3
  151.2 9.1 %fusion.6 = bf16[256,1024]{1,0:T(8,128)(2,1)} fusion(f32[15,1024]{1,0:T(8,128)S(1)} %collective-permute-done.3, f32[15,1024]{1,0:T(8,128)S(1)} %collective-permute-done.2, f32[256,1024]{1,0:T(8,128)S(1)} %subtract_multiply_fusion, f32[256]{0:T(256)S(1)} %get-tuple-element.49, f32[1024]{0:T(1024)S(1)} %bitcast.67, f32[256]{0:T(256)S(1)} %get-tuple-element.50, ...), kind=kLoop, calls=%fused_computation.36 | loop fusion | flops 32243712 | bytes 1854464 | tf_op jit(solution)/shard_map/convert_element_type | solution.py:100
  160.3 198.5 %all-reduce.3.cloned.1.call-done = f32[1024,128]{1,0:T(8,128)} async-done(((f32[1024,128]{1,0:T(8,128)}), f32[1024,128]{1,0:T(8,128)}) %all-reduce.3.cloned.1.call-update) | async-done | bytes 524304
  358.8 1.3 dynamic-slice_multiply_fusion
  (11 shorter events, 0.2 us)
Async XLA Ops:
  7.2 60.0 %copy-start = (bf16[256,1024]{1,0:T(8,128)(2,1)S(1)}, bf16[256,1024]{1,0:T(8,128)(2,1)}, u32[]{:S(2)}) copy-start(bf16[256,1024]{1,0:T(8,128)(2,1)} %param.13) | copy-start | bytes 1572868
  7.2 53.2 %copy-start.1 = (bf16[256,1024]{1,0:T(8,128)(2,1)S(1)}, bf16[256,1024]{1,0:T(8,128)(2,1)}, u32[]{:S(2)}) copy-start(bf16[256,1024]{1,0:T(8,128)(2,1)} %param.7) | copy-start | bytes 1572868
  7.2 69.1 %all-gather.4.cloned.1.call-start = ((), (), s32[]{:S(2)}) async-start(), calls=%async_computation.1 | async-start | bytes 2359296 | tf_op jit(solution)/shard_map/all_gather | solution.py:80
  8.1 52.3 %collective-permute-start = (bf16[15,1024]{1,0:T(8,128)(2,1)S(1)}, bf16[15,1024]{1,0:T(8,128)(2,1)S(1)}, u32[]{:S(2)}, u32[]{:S(2)}) collective-permute-start(bf16[15,1024]{1,0:T(8,128)(2,1)S(1)} %get-tuple-element.15), channel_id=1, source_target_pairs={{0,1},{1,2},{2,3},{3,4},{4,5},{5,6},{6,7},{7,8},{8,9},{9,10},{10,1... | collective-permute-start | bytes 92168 | tf_op jit(solution)/shard_map/ppermute | solution.py:14
  12.3 48.1 %collective-permute-start.1 = (bf16[15,1024]{1,0:T(8,128)(2,1)S(1)}, bf16[15,1024]{1,0:T(8,128)(2,1)S(1)}, u32[]{:S(2)}, u32[]{:S(2)}) collective-permute-start(bf16[15,1024]{1,0:T(8,128)(2,1)S(1)} %get-tuple-element.16), channel_id=1, source_target_pairs={{1,0},{2,1},{3,2},{4,3},{5,4},{6,5},{7,6},{8,7},{9,8},{10,9},{11,1... | collective-permute-start | bytes 92168 | tf_op jit(solution)/shard_map/ppermute | solution.py:15
  17.4 133.8 %reduce-scatter.2.cloned.1.call-start = ((), (), s32[]{:S(2)}) async-start(), calls=%async_computation.2 | async-start | bytes 4718592 | tf_op jit(solution)/shard_map/reduce_scatter | solution.py:104
  70.1 288.7 %all-reduce.3.cloned.1.call-start = ((), (), s32[]{:S(2)}) async-start(), calls=%async_computation.3 | async-start | bytes 1048576
  79.1 20.4 %copy-start.2 = (bf16[1024,1024]{1,0:T(8,128)(2,1)S(1)}, bf16[1024,1024]{1,0:T(8,128)(2,1)}, u32[]{:S(2)}) copy-start(bf16[1024,1024]{1,0:T(8,128)(2,1)} %all-gather.4.cloned.1.call-done) | copy-start | bytes 6291460
  79.5 71.7 %collective-permute-start.2 = (f32[15,1024]{1,0:T(8,128)S(1)}, f32[15,1024]{1,0:T(8,128)S(1)}, u32[]{:S(2)}, u32[]{:S(2)}) collective-permute-start(f32[15,1024]{1,0:T(8,128)S(1)} %get-tuple-element.13), channel_id=1, source_target_pairs={{1,0},{2,1},{3,2},{4,3},{5,4},{6,5},{7,6},{8,7},{9,8},{10,9},{11,1... | collective-permute-start | bytes 184328 | tf_op jit(solution)/shard_map/ppermute | solution.py:15
  97.6 53.7 %collective-permute-start.3 = (f32[15,1024]{1,0:T(8,128)S(1)}, f32[15,1024]{1,0:T(8,128)S(1)}, u32[]{:S(2)}, u32[]{:S(2)}) collective-permute-start(f32[15,1024]{1,0:T(8,128)S(1)} %get-tuple-element.14), channel_id=1, source_target_pairs={{0,1},{1,2},{2,3},{3,4},{4,5},{5,6},{6,7},{7,8},{8,9},{9,10},{10,1... | collective-permute-start | bytes 184328 | tf_op jit(solution)/shard_map/ppermute | solution.py:14
Sparse Core Ops, SparseCore 0:
  17.5 58.7 all-gather.3
  79.7 71.3 reduce-scatter.1
  154.4 204.3 all-reduce.2
where the time goes:
time: 368 us; the launch traced here: 367 us
  waiting for transfers between devices  253 us (69%)
  blocking collectives  39.5 us (11%)
  starting transfers between devices  29.3 us (8%)
  other arithmetic  20.6 us (6%)
  between operations  14.6 us (4%)
  matrix products  7.35 us (2%)
    unnamed x4, waiting for transfers between devices  199 us
    reduce_scatter x1, waiting for transfers between devices, per_device(): lax.psum_scatter(weight_term, 'fsdp', scatter_dimension=1, tiled=True)  50 us
    ppermute x2, starting transfers between devices, extended(): after = lax.ppermute(first, axis, down)  23.1 us
    all_gather x1, blocking collectives, per_device(): lax.all_gather(taps, 'fsdp', axis=1, tiled=True)  17.1 us
    all_gather x1, blocking collectives, per_device(): lax.all_gather(norm_gain, 'fsdp', axis=0, tiled=True)  12 us
    all_gather x1, blocking collectives, per_device(): lax.all_gather(conv_bias, 'fsdp', axis=0, tiled=True)  10.3 us
    convert_element_type x1, other arithmetic, per_device(): frame_grad = grad_values.astype(jnp.bfloat16)  9.09 us
  transfers between devices with their start and end apart: 7, of which 3 were waited for; matrix products, arithmetic and copies ran while one was open for 8% of the time, Pallas kernels for 0%

commit v1 on v0

v1 whole, which is shorter than its diff:
```python
import jax
import jax.numpy as jnp
from jax import lax
from jax.experimental import pallas as pl
from jax.experimental.pallas import tpu as pltpu
from jax.sharding import PartitionSpec as P

MESH = pl.DeviceIdType.MESH
F32 = jnp.float32
BF16 = jnp.bfloat16
N = 8
LANES = 128
ROWS = 256
D = 1024
TAPS = 31
HALO = 16
WIN = ROWS + 2 * HALO
GROUP = 64


def fused(frames, lengths, taps, bias, gain, weight, cot,
          out, fgrad, pgrad,
          pack, gpack, pack_f, tap_all, gain_all, tap_f, gain_f,
          halo, fwin, gwin, off_b, rem_b,
          conv, normed, dfac, inv_b, sum_a, sum_b,
          swished, swt, swt_f, swt_rx, cot_sib, w_all,
          tx1, rx1, acc2, tx2, rx2, tx3, rx3,
          tap_s, tap_r, gain_s, gain_r, halo_s, halo_r, ghalo_s, ghalo_r,
          cot_s, cot_r, swt_s, swt_r, wr_s, wr_r, wl_s, wl_r, ws_s, ws_r,
          r1_s, r1_r, r2_s, r2_r, r3_s, r3_r, loc_s):
    dp = lax.axis_index("dp")
    y = lax.axis_index("fsdp")
    core = dp % 2
    z = (dp // 2) % N
    x = dp // (2 * N)
    a = x * (1 - core) + z * core
    b = z * (1 - core) + x * core

    def chip(a_to, b_to):
        return (a_to * (N - (N - 1) * core) + b_to * (1 + (N - 1) * core)) * 2 + core

    def y_peer(k):
        return (dp, (y + k) % N)

    def a_peer(k):
        return (chip((a + k) % N, b), y)

    def b_peer(k):
        return (chip(a, (b + k) % N), y)

    sibling = (dp + 1 - 2 * core, y)
    place = dp * N + y
    count = 128 * N
    after = (place + 1) % count
    before = (place + count - 1) % count
    next_dev = (after // N, after % N)
    prev_dev = (before // N, before % N)

    def remote(src, dst, send, recv, to):
        return pltpu.make_async_remote_copy(
            src_ref=src, dst_ref=dst, send_sem=send, recv_sem=recv,
            device_id=to, device_id_type=MESH)

    barrier = pltpu.get_barrier_semaphore()
    peers = [sibling, next_dev, prev_dev]
    for k in range(1, N):
        peers += [y_peer(k), a_peer(k), b_peer(k)]
    for peer in peers:
        pl.semaphore_signal(barrier, inc=1, device_id=peer, device_id_type=MESH)

    pack_f[0:TAPS, :] = taps[...].astype(F32)
    pack_f[TAPS:TAPS + 1, :] = bias[...].astype(F32)
    pack[...] = pack_f[...].astype(BF16)
    gpack[...] = jnp.broadcast_to(gain[...].astype(F32), (16, LANES)).astype(BF16)

    ends = lengths[...].astype(F32)
    lane = lax.broadcasted_iota(jnp.int32, (N, LANES), 1)
    row8 = lax.broadcasted_iota(jnp.int32, (N, LANES), 0)
    step = 1
    while step < LANES:
        ends = ends + jnp.where(lane >= step, pltpu.roll(ends, step, 1), 0.0)
        step *= 2
    total = jnp.broadcast_to(jnp.max(ends, axis=1, keepdims=True), (N, LANES))
    before_sum = jnp.where(row8 >= 1, pltpu.roll(total, 1, 0), 0.0)
    step = 1
    while step < N:
        before_sum = before_sum + jnp.where(row8 >= step, pltpu.roll(before_sum, step, 0), 0.0)
        step *= 2
    ends = ends + before_sum - (place * ROWS).astype(F32)
    acc2[0, 0] = ends

    def locate(group, carry):
        base = pl.multiple_of(group * GROUP, GROUP)
        rows = (lax.broadcasted_iota(jnp.int32, (GROUP, LANES), 0) + base).astype(F32)
        start = jnp.full((GROUP, LANES), -1e9, F32)
        stop = jnp.full((GROUP, LANES), 1e9, F32)
        for i in range(N):
            edge = jnp.broadcast_to(acc2[0, 0, i:i + 1, :], (GROUP, LANES))
            passed = edge <= rows
            start = jnp.maximum(start, jnp.where(passed, edge, -1e9))
            stop = jnp.minimum(stop, jnp.where(passed, 1e9, edge))
        first = (-(place * ROWS)).astype(F32)
        start = jnp.maximum(jnp.max(start, axis=1, keepdims=True), first)
        stop = jnp.min(stop, axis=1, keepdims=True)
        off_b[pl.ds(base, GROUP), :] = rows - start
        rem_b[pl.ds(base, GROUP), :] = stop - rows
        return carry

    lax.fori_loop(0, ROWS // GROUP, locate, 0)

    for c in range(N):
        fwin[c, HALO:HALO + ROWS, :] = frames[:, c * LANES:(c + 1) * LANES].astype(F32)

    pl.semaphore_wait(barrier, len(peers))

    order = (4, 3, 5, 2, 6, 1, 7)
    tap_copies = {}
    gain_copies = {}
    for k in order:
        tap_copies[k] = remote(pack, tap_all.at[y], tap_s.at[k - 1], tap_r.at[k - 1], y_peer(k))
        tap_copies[k].start()
    halo_down = remote(frames.at[ROWS - HALO:ROWS], halo.at[0], halo_s.at[0], halo_r.at[0], next_dev)
    halo_up = remote(frames.at[0:HALO], halo.at[1], halo_s.at[1], halo_r.at[1], prev_dev)
    halo_down.start()
    halo_up.start()
    for k in order:
        gain_copies[k] = remote(gpack, gain_all.at[y], gain_s.at[k - 1], gain_r.at[k - 1], y_peer(k))
        gain_copies[k].start()

    half = D // 2
    my_half = pl.ds(pl.multiple_of(core * half, half), half)
    other_half = pl.ds(pl.multiple_of((1 - core) * half, half), half)

    def shard(owner):
        return pl.ds(pl.multiple_of(owner * LANES, LANES), LANES)

    def w_block(owner, rows):
        return w_all.at[rows, shard(owner)]

    right, left = y_peer(1), y_peer(N - 1)
    w_right, w_left, w_side = {}, {}, {}

    def send_right(s):
        owner = (y - (s - 1) + N) % N
        src = weight.at[my_half, :] if s == 1 else w_block(owner, my_half)
        w_right[s] = remote(src, w_block(owner, my_half), wr_s.at[s - 1], wr_r.at[s - 1], right)
        w_right[s].start()

    def send_left(s):
        owner = (y + (s - 1)) % N
        src = weight.at[my_half, :] if s == 1 else w_block(owner, my_half)
        w_left[s] = remote(src, w_block(owner, my_half), wl_s.at[s - 1], wl_r.at[s - 1], left)
        w_left[s].start()

    def send_side(slot, owner):
        w_side[slot] = remote(w_block(owner, my_half), w_block(owner, my_half),
                              ws_s.at[slot], ws_r.at[slot], sibling)
        w_side[slot].start()

    def w_service(s):
        if s <= 4:
            owner = (y - s + N) % N
            remote(w_block(owner, my_half), w_block(owner, my_half),
                   wr_s.at[s - 1], wr_r.at[s - 1], right).wait_recv()
            if s < 4:
                send_right(s + 1)
        if s <= 3:
            owner_l = (y + s) % N
            remote(w_block(owner_l, my_half), w_block(owner_l, my_half),
                   wl_s.at[s - 1], wl_r.at[s - 1], left).wait_recv()
            if s < 3:
                send_left(s + 1)
        if s <= 4:
            send_side(s - 1, (y - s + N) % N)
        if s <= 3:
            send_side(4 + s - 1, (y + s) % N)

    send_right(1)
    send_left(1)
    cot_copy = remote(cot, cot_sib, cot_s, cot_r, sibling)
    cot_copy.start()
    own_w = pltpu.make_async_copy(weight, w_all.at[:, shard(y)], loc_s)
    own_w.start()

    tap_f[y] = pack[...].astype(F32)
    for k in range(1, N):
        source = (y - k + N) % N
        remote(tap_all.at[source], tap_all.at[source], tap_s.at[k - 1], tap_r.at[k - 1],
               y_peer(N - k)).wait_recv()
        tap_f[source] = tap_all[source].astype(F32)
    halo_down.wait_recv()
    halo_up.wait_recv()
    for c in range(N):
        fwin[c, 0:HALO, :] = halo[0, :, c * LANES:(c + 1) * LANES].astype(F32)
        fwin[c, HALO + ROWS:WIN, :] = halo[1, :, c * LANES:(c + 1) * LANES].astype(F32)

    def convolve(window, pair, base, reverse):
        off = off_b[pl.ds(base, GROUP), :]
        rem = rem_b[pl.ds(base, GROUP), :]
        sums = []
        for c in pair:
            if reverse:
                sums.append(jnp.zeros((GROUP, LANES), F32))
            else:
                sums.append(jnp.broadcast_to(tap_f[c, TAPS:TAPS + 1, :], (GROUP, LANES)))
        for j in range(TAPS):
            d = j - (TAPS - 1) // 2
            together = off >= float(-d) if d < 0 else rem > float(d)
            tap = TAPS - 1 - j if reverse else j
            for i, c in enumerate(pair):
                value = window[c, pl.ds(base + (j + 1), GROUP), :]
                if d != 0:
                    value = jnp.where(together, value, 0.0)
                sums[i] = sums[i] + tap_f[c, tap:tap + 1, :] * value
        return sums

    def forward_pair(p):
        def body(group, carry):
            base = pl.multiple_of(group * GROUP, GROUP)
            one, two = convolve(fwin, (2 * p, 2 * p + 1), base, False)
            conv[2 * p, pl.ds(base, GROUP), :] = one
            conv[2 * p + 1, pl.ds(base, GROUP), :] = two
            return carry

        lax.fori_loop(0, ROWS // GROUP, body, 0)

    for p in range(4):
        forward_pair(p)
        if p == 2:
            w_service(1)

    def over_features(make):
        def body(group, carry):
            base = pl.multiple_of(group * GROUP, GROUP)
            rows = pl.ds(base, GROUP)
            sum_a[rows, :] = make(rows)
            return carry

        lax.fori_loop(0, ROWS // GROUP, body, 0)
        return jnp.sum(sum_a[...], axis=1, keepdims=True) * (1.0 / D)

    def plain(rows):
        total = conv[0, rows, :]
        for c in range(1, N):
            total = total + conv[c, rows, :]
        return total

    sum_b[...] = jnp.broadcast_to(over_features(plain), (ROWS, LANES))

    def squares(rows):
        mean = sum_b[rows, :]
        total = jnp.zeros((GROUP, LANES), F32)
        for c in range(N):
            centre = conv[c, rows, :] - mean
            total = total + centre * centre
        return total

    inv_b[...] = jnp.broadcast_to(lax.rsqrt(over_features(squares) + 1e-05), (ROWS, LANES))

    gain_f[y] = gpack[...].astype(F32)
    for k in range(1, N):
        source = (y - k + N) % N
        remote(gain_all.at[source], gain_all.at[source], gain_s.at[k - 1], gain_r.at[k - 1],
               y_peer(N - k)).wait_recv()
        gain_f[source] = gain_all[source].astype(F32)

    def swish_block(c, carry):
        gain_row = gain_f[c, 0:1, :]
        for h in range(2):
            rows = pl.ds(h * 128, 128)
            unit = (conv[c, rows, :] - sum_b[rows, :]) * inv_b[rows, :]
            normed[c, rows, :] = unit
            scaled = unit * gain_row
            gate = 1.0 / (1.0 + jnp.exp(-scaled))
            sw = (scaled * gate).astype(BF16)
            dfac[c, rows, :] = (gate + scaled * gate * (1.0 - gate)) * gain_row
            swished[rows, shard(c)] = sw
            turned = jnp.transpose(sw.astype(F32)).reshape(N, 2, 8, 128)
            swt[0, c, :, h * 128:(h + 1) * 128] = turned[:, 0].reshape(64, 128).astype(BF16)
            swt_f[:, c, :, h * 128:(h + 1) * 128] = turned[:, 1]
        return carry

    lax.fori_loop(0, N, swish_block, 0)
    for i in range(N):
        swt[1, i] = swt_f[i].reshape(64, ROWS).astype(BF16)

    swt_copy = remote(swt.at[1 - core], swt_rx, swt_s, swt_r, sibling)
    swt_copy.start()
    w_service(2)
    cot_copy.wait_recv()
    swt_copy.wait_recv()

    for n in range(4):
        cols = slice(n * 256, (n + 1) * 256)
        part = jnp.dot(swt[core].reshape(512, ROWS), cot[:, cols], preferred_element_type=F32)
        part = part + jnp.dot(swt_rx[...].reshape(512, ROWS), cot_sib[:, cols], preferred_element_type=F32)
        tx1[:, :, cols] = part.astype(BF16).reshape(N, 64, 256)

    r1 = {}
    for k in order:
        r1[k] = remote(tx1.at[(a + k) % N], rx1.at[k - 1], r1_s.at[k - 1], r1_r.at[k - 1], a_peer(k))
        r1[k].start()

    w_service(3)
    w_service(4)
    own_w.wait()
    for s in range(1, 5):
        owner = (y - s + N) % N
        remote(w_block(owner, other_half), w_block(owner, other_half),
               ws_s.at[s - 1], ws_r.at[s - 1], sibling).wait_recv()
    for s in range(1, 4):
        owner = (y + s) % N
        remote(w_block(owner, other_half), w_block(owner, other_half),
               ws_s.at[4 + s - 1], ws_r.at[4 + s - 1], sibling).wait_recv()

    sum_a[...] = jnp.zeros((ROWS, LANES), F32)
    sum_b[...] = jnp.zeros((ROWS, LANES), F32)
    for n in range(4):
        grad = lax.dot_general(cot[...], w_all[n * 256:(n + 1) * 256, :], (((1,), (1,)), ((), ())),
                               preferred_element_type=F32)
        for i in range(2):
            c = 2 * n + i
            grad_normed = grad[:, i * LANES:(i + 1) * LANES] * dfac[c]
            gwin[c, HALO:HALO + ROWS, :] = grad_normed
            sum_a[...] += grad_normed
            sum_b[...] += grad_normed * normed[c]
    sum_a[...] = jnp.broadcast_to(jnp.sum(sum_a[...], axis=1, keepdims=True) * (1.0 / D), (ROWS, LANES))
    sum_b[...] = jnp.broadcast_to(jnp.sum(sum_b[...], axis=1, keepdims=True) * (1.0 / D), (ROWS, LANES))

    def norm_back(c, carry):
        gwin[c, HALO:HALO + ROWS, :] = inv_b[...] * (
            gwin[c, HALO:HALO + ROWS, :] - sum_a[...] - normed[c] * sum_b[...])
        return carry

    lax.fori_loop(0, N, norm_back, 0)

    ghalo_down = remote(gwin.at[:, ROWS:ROWS + HALO, :], gwin.at[:, 0:HALO, :],
                        ghalo_s.at[0], ghalo_r.at[0], next_dev)
    ghalo_up = remote(gwin.at[:, HALO:2 * HALO, :], gwin.at[:, ROWS + HALO:WIN, :],
                      ghalo_s.at[1], ghalo_r.at[1], prev_dev)
    ghalo_down.start()
    ghalo_up.start()

    for n in range(4):
        cols = slice(n * 256, (n + 1) * 256)
        out[:, cols] = jnp.dot(swished[...], w_all[:, cols], preferred_element_type=F32).astype(BF16)

    ghalo_down.wait_recv()
    ghalo_up.wait_recv()

    def backward_pair(p):
        def body(group, carry):
            base = pl.multiple_of(group * GROUP, GROUP)
            pair = convolve(gwin, (2 * p, 2 * p + 1), base, True)
            for i in range(2):
                c = 2 * p + i
                fgrad[pl.ds(base, GROUP), c * LANES:(c + 1) * LANES] = pair[i].astype(BF16)
            return carry

        lax.fori_loop(0, ROWS // GROUP, body, 0)

    def reduce_a():
        for k in range(1, N):
            remote(tx1.at[0], rx1.at[k - 1], r1_s.at[k - 1], r1_r.at[k - 1], a_peer(N - k)).wait_recv()
        for c in range(N):
            cols = slice(c * LANES, (c + 1) * LANES)
            total = tx1[a, :, cols].astype(F32)
            for k in range(1, N):
                total = total + rx1[k - 1, :, cols].astype(F32)
            acc2[:, c] = total.reshape(N, 8, LANES)
        for i in range(N):
            tx2[i] = acc2[i].reshape(64, LANES).astype(BF16)
        for k in order:
            remote(tx2.at[(b + k) % N], rx2.at[k - 1], r2_s.at[k - 1], r2_r.at[k - 1], b_peer(k)).start()

    def reduce_b():
        for k in range(1, N):
            remote(tx2.at[0], rx2.at[k - 1], r2_s.at[k - 1], r2_r.at[k - 1], b_peer(N - k)).wait_recv()
        total = acc2[b].reshape(64, LANES)
        for k in range(1, N):
            total = total + rx2[k - 1].astype(F32)
        tx3[...] = total.reshape(N, 8, LANES)
        for k in order:
            remote(tx3.at[(y + k) % N], rx3.at[k - 1], r3_s.at[k - 1], r3_r.at[k - 1], y_peer(k)).start()

    def reduce_y():
        for k in range(1, N):
            remote(tx3.at[0], rx3.at[k - 1], r3_s.at[k - 1], r3_r.at[k - 1], y_peer(N - k)).wait_recv()
        total = tx3[y]
        for k in range(1, N):
            total = total + rx3[k - 1]
        pgrad[...] = total * (1.0 / 1024)

    backward_pair(0)
    backward_pair(1)
    reduce_a()
    backward_pair(2)
    reduce_b()
    backward_pair(3)
    reduce_y()

    for k in range(1, N):
        tap_copies[k].wait_send()
        gain_copies[k].wait_send()
        r1[k].wait_send()
        remote(tx2.at[0], rx2.at[k - 1], r2_s.at[k - 1], r2_r.at[k - 1], b_peer(k)).wait_send()
        remote(tx3.at[0], rx3.at[k - 1], r3_s.at[k - 1], r3_r.at[k - 1], y_peer(k)).wait_send()
    for copy in (halo_down, halo_up, ghalo_down, ghalo_up, cot_copy, swt_copy):
        copy.wait_send()
    for copies in (w_right, w_left, w_side):
        for copy in copies.values():
            copy.wait_send()


def per_device(frames, lengths, taps, conv_bias, norm_gain, proj_weight, cotangent):
    vmem = pl.BlockSpec(memory_space=pltpu.VMEM)
    dma = pltpu.SemaphoreType.DMA
    scratch = [
        pltpu.VMEM((32, LANES), BF16), pltpu.VMEM((16, LANES), BF16), pltpu.VMEM((32, LANES), F32),
        pltpu.VMEM((N, 32, LANES), BF16), pltpu.VMEM((N, 16, LANES), BF16),
        pltpu.VMEM((N, 32, LANES), F32), pltpu.VMEM((N, 16, LANES), F32),
        pltpu.VMEM((2, HALO, D), BF16),
        pltpu.VMEM((N, WIN, LANES), F32), pltpu.VMEM((N, WIN, LANES), F32),
        pltpu.VMEM((ROWS, LANES), F32), pltpu.VMEM((ROWS, LANES), F32),
        pltpu.VMEM((N, ROWS, LANES), F32), pltpu.VMEM((N, ROWS, LANES), F32),
        pltpu.VMEM((N, ROWS, LANES), F32),
        pltpu.VMEM((ROWS, LANES), F32), pltpu.VMEM((ROWS, LANES), F32), pltpu.VMEM((ROWS, LANES), F32),
        pltpu.VMEM((ROWS, D), BF16),
        pltpu.VMEM((2, N, 64, ROWS), BF16), pltpu.VMEM((N, N, 8, ROWS), F32), pltpu.VMEM((N, 64, ROWS), BF16),
        pltpu.VMEM((ROWS, D), BF16), pltpu.VMEM((D, D), BF16),
        pltpu.VMEM((N, 64, D), BF16), pltpu.VMEM((N - 1, 64, D), BF16),
        pltpu.VMEM((N, N, 8, LANES), F32),
        pltpu.VMEM((N, 64, LANES), BF16), pltpu.VMEM((N - 1, 64, LANES), BF16),
        pltpu.VMEM((N, 8, LANES), F32), pltpu.VMEM((N - 1, 8, LANES), F32),
        dma((7,)), dma((7,)), dma((7,)), dma((7,)), dma((2,)), dma((2,)), dma((2,)), dma((2,)),
        dma, dma, dma, dma, dma((4,)), dma((4,)), dma((3,)), dma((3,)), dma((7,)), dma((7,)),
        dma((7,)), dma((7,)), dma((7,)), dma((7,)), dma((7,)), dma((7,)), dma,
    ]
    return pl.pallas_call(
        fused,
        out_shape=(
            jax.ShapeDtypeStruct((ROWS, D), BF16),
            jax.ShapeDtypeStruct((ROWS, D), BF16),
            jax.ShapeDtypeStruct((8, LANES), F32),
        ),
        in_specs=[vmem] * 7,
        out_specs=(vmem, vmem, vmem),
        scratch_shapes=scratch,
        compiler_params=pltpu.CompilerParams(
            collective_id=0, has_side_effects=True, vmem_limit_bytes=40 * 1024 * 1024),
        name="fused_module",
    )(frames, lengths.reshape(N, LANES), taps, conv_bias.reshape(1, LANES),
      norm_gain.reshape(1, LANES), proj_weight, cotangent)


def solution(mesh):
    rows = P(("dp", "fsdp"), None)
    in_specs = (rows, P(), P(None, "fsdp"), P("fsdp"), P("fsdp"), P(None, "fsdp"), rows)
    out_specs = (rows, rows, P("dp", "fsdp"))
    return jax.shard_map(
        per_device, mesh=mesh, in_specs=in_specs, out_specs=out_specs, check_vma=False)
```

time: 368 us -> 70 us (0.19)
  waiting for transfers between devices: 253 us -> 0 us
  Pallas kernels: 0 us -> 62.4 us
  blocking collectives: 39.5 us -> 0 us
  starting transfers between devices: 29.3 us -> 0 us
  other arithmetic: 20.6 us -> 0 us
  between operations: 14.6 us -> 0.67 us
  matrix products: 7.35 us -> 0 us
  local copies, waits for them, and re-layouts: 2.46 us -> 6.58 us
    unnamed x4 -> x0, waiting for transfers between devices: 199 us -> none
    pallas_call x0 -> x1, Pallas kernels: none -> 62.4 us  [per_device(): pl.pallas_call(fused, out_shape=(jax.ShapeDtypeStruct((ROWS, D), BF16), j...]
    reduce_scatter x1 -> x0, waiting for transfers between devices: 50 us -> none  [per_device(): lax.psum_scatter(weight_term, 'fsdp', scatter_dimension=1, tiled=True)]
    all_gather x3 -> x0, blocking collectives: 39.5 us -> none  [the longest x1 17.1 us: per_device(): lax.all_gather(taps, 'fsdp', axis=1, tiled=True)]
    ppermute x4 -> x0, starting transfers between devices: 29.2 us -> none  [the longest x2 23.1 us: extended(): after = lax.ppermute(first, axis, down)]
    convert_element_type x6 -> x0, other arithmetic: 9.31 us -> none  [the longest x1 9.09 us: per_device(): frame_grad = grad_values.astype(jnp.bfloat16)]
    reduce_sum x4 -> x0, other arithmetic: 7.89 us -> none  [the longest x1 6.26 us: forward(): centre = conv_out - jnp.mean(conv_out, axis=-1, keepdims=True)]
    dot_general x3 -> x0, matrix products: 7.35 us -> none  [the longest x1 2.89 us: per_device(): lax.dot_general(swished_mid, cotangent, (((0,), (0,)), ((), ())), preferr...]
  transfers between devices with their start and end apart: 7 -> 0, of which waited for: 3 -> 0; matrix products, arithmetic and copies ran while one was open for 8% -> 0% of each run, Pallas kernels for 0% -> 0%
where the time goes in v1:
time: 70 us; the launch traced here: 69.7 us
  Pallas kernels  62.4 us (89%)
  local copies, waits for them, and re-layouts  6.58 us (9%)
    pallas_call x1, Pallas kernels, per_device(): pl.pallas_call(fused, out_shape=(jax.ShapeDtypeStruct((ROWS, D), BF16), j...  62.4 us
    unnamed x17, local copies, waits for them, and re-layouts  6.58 us

profile of v1, /device:TPU:1, one launch (start us, length us, event | category | flops | bytes accessed | tf_op | source)
XLA Modules:
  0.0 69.7 jit_solution(3706858221380618480)
XLA Ops:
  0.6 0.0 copy-start.4
  0.6 0.0 copy-start.5
  0.7 0.0 copy-start.6
  0.7 0.7 copy-done.4
  1.3 0.0 copy-done.5
  1.3 0.0 copy-done.6
  1.3 0.0 copy-start
  1.3 1.0 %copy-done = bf16[256,1024]{1,0:T(8,128)(2,1)S(1)} copy-done((bf16[256,1024]{1,0:T(8,128)(2,1)S(1)}, bf16[256,1024]{1,0:T(8,128)(2,1)}, u32[]{:S(2)}) %copy-start) | copy-done | bytes 524312
  2.4 0.0 copy-start.1
  2.4 1.0 %copy-done.1 = bf16[256,1024]{1,0:T(8,128)(2,1)S(1)} copy-done((bf16[256,1024]{1,0:T(8,128)(2,1)S(1)}, bf16[256,1024]{1,0:T(8,128)(2,1)}, u32[]{:S(2)}) %copy-start.1) | copy-done | bytes 524312
  3.4 0.0 copy-start.2
  3.4 0.9 %copy-done.2 = bf16[1024,128]{1,0:T(8,128)(2,1)S(1)} copy-done((bf16[1024,128]{1,0:T(8,128)(2,1)S(1)}, bf16[1024,128]{1,0:T(8,128)(2,1)}, u32[]{:S(2)}) %copy-start.2) | copy-done | bytes 262168
  4.4 0.0 copy-start.3
  4.4 0.7 copy-done.3
  5.1 62.4 %fused_module.1 = (bf16[256,1024]{1,0:T(8,128)(2,1)S(1)}, bf16[256,1024]{1,0:T(8,128)(2,1)S(1)}, f32[8,128]{1,0:T(8,128)S(1)}) custom-call(bf16[256,1024]{1,0:T(8,128)(2,1)S(1)} %copy-done, s32[8,128]{1,0:T(8,128)S(1)} %bitcast.3, bf16[31,128]{1,0:T(8,128)(2,1)S(1)} %copy-done.3, bf16[1,128]{1,0:T(2,128)(2,1)S(1)} %bitcast.4, bf16[1,128]{1,0:T(2,128)(2,1)S(1)} %bitcast.5, ...), custom_call_target="tpu_custom_call" | custom-call | tf_op jit(solution)/shard_map/fused_module/pallas_call | solution.py:439
  67.5 0.8 %copy.13 = bf16[256,1024]{1,0:T(8,128)(2,1)} copy(bf16[256,1024]{1,0:T(8,128)(2,1)S(1)} %get-tuple-element.6) | data formatting | bytes 1048576
  68.3 0.8 %copy.14 = bf16[256,1024]{1,0:T(8,128)(2,1)} copy(bf16[256,1024]{1,0:T(8,128)(2,1)S(1)} %get-tuple-element.7) | data formatting | bytes 1048576
  69.1 0.6 copy.15
Async XLA Ops:
  0.6 0.7 copy-start.4
  0.6 0.7 copy-start.5
  0.7 0.7 copy-start.6
  1.3 1.0 %copy-start = (bf16[256,1024]{1,0:T(8,128)(2,1)S(1)}, bf16[256,1024]{1,0:T(8,128)(2,1)}, u32[]{:S(2)}) copy-start(bf16[256,1024]{1,0:T(8,128)(2,1)} %frames.1) | copy-start | bytes 1572868
  2.4 1.0 %copy-start.1 = (bf16[256,1024]{1,0:T(8,128)(2,1)S(1)}, bf16[256,1024]{1,0:T(8,128)(2,1)}, u32[]{:S(2)}) copy-start(bf16[256,1024]{1,0:T(8,128)(2,1)} %cot.1) | copy-start | bytes 1572868
  3.4 0.9 %copy-start.2 = (bf16[1024,128]{1,0:T(8,128)(2,1)S(1)}, bf16[1024,128]{1,0:T(8,128)(2,1)}, u32[]{:S(2)}) copy-start(bf16[1024,128]{1,0:T(8,128)(2,1)} %weight.1) | copy-start | bytes 786436
  4.4 0.7 %copy-start.3 = (bf16[31,128]{1,0:T(8,128)(2,1)S(1)}, bf16[31,128]{1,0:T(8,128)(2,1)}, u32[]{:S(2)}) copy-start(bf16[31,128]{1,0:T(8,128)(2,1)} %taps.1) | copy-start | bytes 23812

commit v2 on v1

--- a/solution.py
+++ b/solution.py
@@ -18,8 +18,9 @@
 GROUP = 64
 
 
-def fused(frames, lengths, taps, bias, gain, weight, cot,
-          out, fgrad, pgrad,
+def fused(frames_h, lengths_h, taps_h, bias_h, gain_h, weight, cot_h,
+          out_h, fgrad_h, pgrad_h,
+          out, fgrad, pgrad, frames, lengths, taps, bias, gain, cot,
           pack, gpack, pack_f, tap_all, gain_all, tap_f, gain_f,
           halo, fwin, gwin, off_b, rem_b,
           conv, normed, dfac, inv_b, sum_a, sum_b,
@@ -27,7 +28,7 @@
           tx1, rx1, acc2, tx2, rx2, tx3, rx3,
           tap_s, tap_r, gain_s, gain_r, halo_s, halo_r, ghalo_s, ghalo_r,
           cot_s, cot_r, swt_s, swt_r, wr_s, wr_r, wl_s, wl_r, ws_s, ws_r,
-          r1_s, r1_r, r2_s, r2_r, r3_s, r3_r, loc_s):
+          r1_s, r1_r, r2_s, r2_r, r3_s, r3_r, loc_s, done_s):
     dp = lax.axis_index("dp")
     y = lax.axis_index("fsdp")
     core = dp % 2
@@ -61,17 +62,99 @@
             src_ref=src, dst_ref=dst, send_sem=send, recv_sem=recv,
             device_id=to, device_id_type=MESH)
 
+    loads = [pltpu.make_async_copy(src, dst, loc_s.at[i]) for i, (src, dst) in enumerate((
+        (lengths_h, lengths), (taps_h, taps), (bias_h, bias), (gain_h, gain), (frames_h, frames), (cot_h, cot)))]
+    for load in loads:
+        load.start()
+
     barrier = pltpu.get_barrier_semaphore()
-    peers = [sibling, next_dev, prev_dev]
-    for k in range(1, N):
-        peers += [y_peer(k), a_peer(k), b_peer(k)]
+    order = (4, 3, 5, 2, 6, 1, 7)
+    peers = [y_peer(k) for k in order] + [next_dev, prev_dev, sibling]
+    for k in order:
+        peers += [a_peer(k), b_peer(k)]
     for peer in peers:
         pl.semaphore_signal(barrier, inc=1, device_id=peer, device_id_type=MESH)
+
+    for load in loads[:4]:
+        load.wait()
 
     pack_f[0:TAPS, :] = taps[...].astype(F32)
     pack_f[TAPS:TAPS + 1, :] = bias[...].astype(F32)
     pack[...] = pack_f[...].astype(BF16)
     gpack[...] = jnp.broadcast_to(gain[...].astype(F32), (16, LANES)).astype(BF16)
+
+    pl.semaphore_wait(barrier, len(peers))
+
+    near = (1, 7, 2, 6, 3, 5, 4)
+    tap_copies = {}
+    gain_copies = {}
+    for k in near:
+        tap_copies[k] = remote(pack, tap_all.at[y], tap_s.at[k - 1], tap_r.at[k - 1], y_peer(k))
+        tap_copies[k].start()
+    halo_down = remote(frames_h.at[ROWS - HALO:ROWS], halo.at[0], halo_s.at[0], halo_r.at[0], next_dev)
+    halo_up = remote(frames_h.at[0:HALO], halo.at[1], halo_s.at[1], halo_r.at[1], prev_dev)
+    halo_down.start()
+    halo_up.start()
+    half = D // 2
+    my_half = pl.ds(pl.multiple_of(core * half, half), half)
+    other_half = pl.ds(pl.multiple_of((1 - core) * half, half), half)
+
+    def shard(owner):
+        return pl.ds(pl.multiple_of(owner * LANES, LANES), LANES)
+
+    def w_block(owner, rows):
+        return w_all.at[rows, shard(owner)]
+
+    right, left = y_peer(1), y_peer(N - 1)
+    w_right, w_left, w_side = {}, {}, {}
+
+    quarter = half // 2
+    first_part = pl.ds(pl.multiple_of(core * half, quarter), quarter)
+    second_part = pl.ds(pl.multiple_of(core * half + quarter, quarter), quarter)
+
+    def send_right(s):
+        owner = (y - (s - 1) + N) % N
+        rows = first_part if s == 4 else my_half
+        src = weight.at[rows, :] if s == 1 else w_block(owner, rows)
+        w_right[s] = remote(src, w_block(owner, rows), wr_s.at[s - 1], wr_r.at[s - 1], right)
+        w_right[s].start()
+
+    def send_left(s):
+        owner = (y + (s - 1)) % N
+        rows = second_part if s == 4 else my_half
+        src = weight.at[rows, :] if s == 1 else w_block(owner, rows)
+        w_left[s] = remote(src, w_block(owner, rows), wl_s.at[s - 1], wl_r.at[s - 1], left)
+        w_left[s].start()
+
+    def send_side(slot, owner):
+        w_side[slot] = remote(w_block(owner, my_half), w_block(owner, my_half),
+                              ws_s.at[slot], ws_r.at[slot], sibling)
+        w_side[slot].start()
+
+    def w_service(s):
+        below, above = (y - s + N) % N, (y + s) % N
+        rows = first_part if s == 4 else my_half
+        remote(w_block(below, rows), w_block(below, rows), wr_s.at[s - 1], wr_r.at[s - 1], right).wait_recv()
+        if s < 4:
+            send_right(s + 1)
+            send_side(s - 1, below)
+        rows = second_part if s == 4 else my_half
+        remote(w_block(above, rows), w_block(above, rows), wl_s.at[s - 1], wl_r.at[s - 1], left).wait_recv()
+        if s < 4:
+            send_left(s + 1)
+            send_side(3 + s, above)
+        else:
+            send_side(3, below)
+
+    for k in near:
+        gain_copies[k] = remote(gpack, gain_all.at[y], gain_s.at[k - 1], gain_r.at[k - 1], y_peer(k))
+        gain_copies[k].start()
+    send_right(1)
+    send_left(1)
+    cot_copy = remote(cot_h, cot_sib, cot_s, cot_r, sibling)
+    cot_copy.start()
+    own_w = pltpu.make_async_copy(weight, w_all.at[:, shard(y)], loc_s.at[6])
+    own_w.start()
 
     ends = lengths[...].astype(F32)
     lane = lax.broadcasted_iota(jnp.int32, (N, LANES), 1)
@@ -108,97 +191,22 @@
 
     lax.fori_loop(0, ROWS // GROUP, locate, 0)
 
+    loads[4].wait()
     for c in range(N):
         fwin[c, HALO:HALO + ROWS, :] = frames[:, c * LANES:(c + 1) * LANES].astype(F32)
 
-    pl.semaphore_wait(barrier, len(peers))
-
-    order = (4, 3, 5, 2, 6, 1, 7)
-    tap_copies = {}
-    gain_copies = {}
-    for k in order:
-        tap_copies[k] = remote(pack, tap_all.at[y], tap_s.at[k - 1], tap_r.at[k - 1], y_peer(k))
-        tap_copies[k].start()
-    halo_down = remote(frames.at[ROWS - HALO:ROWS], halo.at[0], halo_s.at[0], halo_r.at[0], next_dev)
-    halo_up = remote(frames.at[0:HALO], halo.at[1], halo_s.at[1], halo_r.at[1], prev_dev)
-    halo_down.start()
-    halo_up.start()
-    for k in order:
-        gain_copies[k] = remote(gpack, gain_all.at[y], gain_s.at[k - 1], gain_r.at[k - 1], y_peer(k))
-        gain_copies[k].start()
-
-    half = D // 2
-    my_half = pl.ds(pl.multiple_of(core * half, half), half)
-    other_half = pl.ds(pl.multiple_of((1 - core) * half, half), half)
-
-    def shard(owner):
-        return pl.ds(pl.multiple_of(owner * LANES, LANES), LANES)
-
-    def w_block(owner, rows):
-        return w_all.at[rows, shard(owner)]
-
-    right, left = y_peer(1), y_peer(N - 1)
-    w_right, w_left, w_side = {}, {}, {}
-
-    def send_right(s):
-        owner = (y - (s - 1) + N) % N
-        src = weight.at[my_half, :] if s == 1 else w_block(owner, my_half)
-        w_right[s] = remote(src, w_block(owner, my_half), wr_s.at[s - 1], wr_r.at[s - 1], right)
-        w_right[s].start()
-
-    def send_left(s):
-        owner = (y + (s - 1)) % N
-        src = weight.at[my_half, :] if s == 1 else w_block(owner, my_half)
-        w_left[s] = remote(src, w_block(owner, my_half), wl_s.at[s - 1], wl_r.at[s - 1], left)
-        w_left[s].start()
-
-    def send_side(slot, owner):
-        w_side[slot] = remote(w_block(owner, my_half), w_block(owner, my_half),
-                              ws_s.at[slot], ws_r.at[slot], sibling)
-        w_side[slot].start()
-
-    def w_service(s):
-        if s <= 4:
-            owner = (y - s + N) % N
-            remote(w_block(owner, my_half), w_block(owner, my_half),
-                   wr_s.at[s - 1], wr_r.at[s - 1], right).wait_recv()
-            if s < 4:
-                send_right(s + 1)
-        if s <= 3:
-            owner_l = (y + s) % N
-            remote(w_block(owner_l, my_half), w_block(owner_l, my_half),
-                   wl_s.at[s - 1], wl_r.at[s - 1], left).wait_recv()
-            if s < 3:
-                send_left(s + 1)
-        if s <= 4:
-            send_side(s - 1, (y - s + N) % N)
-        if s <= 3:
-            send_side(4 + s - 1, (y + s) % N)
-
-    send_right(1)
-    send_left(1)
-    cot_copy = remote(cot, cot_sib, cot_s, cot_r, sibling)
-    cot_copy.start()
-    own_w = pltpu.make_async_copy(weight, w_all.at[:, shard(y)], loc_s)
-    own_w.start()
-
-    tap_f[y] = pack[...].astype(F32)
-    for k in range(1, N):
+    def tap_arrives(k):
         source = (y - k + N) % N
         remote(tap_all.at[source], tap_all.at[source], tap_s.at[k - 1], tap_r.at[k - 1],
                y_peer(N - k)).wait_recv()
         tap_f[source] = tap_all[source].astype(F32)
-    halo_down.wait_recv()
-    halo_up.wait_recv()
-    for c in range(N):
-        fwin[c, 0:HALO, :] = halo[0, :, c * LANES:(c + 1) * LANES].astype(F32)
-        fwin[c, HALO + ROWS:WIN, :] = halo[1, :, c * LANES:(c + 1) * LANES].astype(F32)
-
-    def convolve(window, pair, base, reverse):
+        return source
+
+    def convolve(window, blocks, base, reverse):
         off = off_b[pl.ds(base, GROUP), :]
         rem = rem_b[pl.ds(base, GROUP), :]
         sums = []
-        for c in pair:
+        for c in blocks:
             if reverse:
                 sums.append(jnp.zeros((GROUP, LANES), F32))
             else:
@@ -207,27 +215,38 @@
             d = j - (TAPS - 1) // 2
             together = off >= float(-d) if d < 0 else rem > float(d)
             tap = TAPS - 1 - j if reverse else j
-            for i, c in enumerate(pair):
+            for i, c in enumerate(blocks):
                 value = window[c, pl.ds(base + (j + 1), GROUP), :]
                 if d != 0:
                     value = jnp.where(together, value, 0.0)
                 sums[i] = sums[i] + tap_f[c, tap:tap + 1, :] * value
         return sums
 
-    def forward_pair(p):
+    def forward_blocks(blocks, first, count, stride):
         def body(group, carry):
-            base = pl.multiple_of(group * GROUP, GROUP)
-            one, two = convolve(fwin, (2 * p, 2 * p + 1), base, False)
-            conv[2 * p, pl.ds(base, GROUP), :] = one
-            conv[2 * p + 1, pl.ds(base, GROUP), :] = two
+            base = pl.multiple_of(first + group * stride, GROUP)
+            for c, value in zip(blocks, convolve(fwin, blocks, base, False)):
+                conv[c, pl.ds(base, GROUP), :] = value
             return carry
 
-        lax.fori_loop(0, ROWS // GROUP, body, 0)
-
-    for p in range(4):
-        forward_pair(p)
-        if p == 2:
-            w_service(1)
+        lax.fori_loop(0, count, body, 0)
+
+    tap_f[y] = pack[...].astype(F32)
+    forward_blocks((y,), GROUP, 2, GROUP)
+    blocks = (tap_arrives(1), tap_arrives(7))
+    forward_blocks(blocks, GROUP, 2, GROUP)
+    halo_down.wait_recv()
+    halo_up.wait_recv()
+    for c in range(N):
+        fwin[c, 0:HALO, :] = halo[0, :, c * LANES:(c + 1) * LANES].astype(F32)
+        fwin[c, HALO + ROWS:WIN, :] = halo[1, :, c * LANES:(c + 1) * LANES].astype(F32)
+    forward_blocks(blocks, 0, 2, ROWS - GROUP)
+    forward_blocks((tap_arrives(2), tap_arrives(6)), 0, 4, GROUP)
+    w_service(1)
+    forward_blocks((tap_arrives(3), tap_arrives(5)), 0, 4, GROUP)
+    last = tap_arrives(4)
+    forward_blocks((y, last), 0, 2, ROWS - GROUP)
+    forward_blocks((last,), GROUP, 2, GROUP)
 
     def over_features(make):
         def body(group, carry):
@@ -286,7 +305,7 @@
 
     swt_copy = remote(swt.at[1 - core], swt_rx, swt_s, swt_r, sibling)
     swt_copy.start()
-    w_service(2)
+    loads[5].wait()
     cot_copy.wait_recv()
     swt_copy.wait_recv()
 
@@ -301,6 +320,7 @@
         r1[k] = remote(tx1.at[(a + k) % N], rx1.at[k - 1], r1_s.at[k - 1], r1_r.at[k - 1], a_peer(k))
         r1[k].start()
 
+    w_service(2)
     w_service(3)
     w_service(4)
     own_w.wait()
@@ -344,20 +364,19 @@
     for n in range(4):
         cols = slice(n * 256, (n + 1) * 256)
         out[:, cols] = jnp.dot(swished[...], w_all[:, cols], preferred_element_type=F32).astype(BF16)
-
-    ghalo_down.wait_recv()
-    ghalo_up.wait_recv()
-
-    def backward_pair(p):
+    writes = [pltpu.make_async_copy(out, out_h, done_s.at[0])]
+    writes[0].start()
+
+    def backward_pair(p, first, count, stride):
         def body(group, carry):
-            base = pl.multiple_of(group * GROUP, GROUP)
+            base = pl.multiple_of(first + group * stride, GROUP)
             pair = convolve(gwin, (2 * p, 2 * p + 1), base, True)
             for i in range(2):
                 c = 2 * p + i
                 fgrad[pl.ds(base, GROUP), c * LANES:(c + 1) * LANES] = pair[i].astype(BF16)
             return carry
 
-        lax.fori_loop(0, ROWS // GROUP, body, 0)
+        lax.fori_loop(0, count, body, 0)
 
     def reduce_a():
         for k in range(1, N):
@@ -390,13 +409,20 @@
         for k in range(1, N):
             total = total + rx3[k - 1]
         pgrad[...] = total * (1.0 / 1024)
-
-    backward_pair(0)
-    backward_pair(1)
+        writes.append(pltpu.make_async_copy(pgrad, pgrad_h, done_s.at[5]))
+        writes[-1].start()
+
+    for p in range(4):
+        backward_pair(p, GROUP, 2, GROUP)
     reduce_a()
-    backward_pair(2)
+    ghalo_down.wait_recv()
+    ghalo_up.wait_recv()
+    for p in range(4):
+        backward_pair(p, 0, 2, ROWS - GROUP)
+        cols = slice(p * 256, (p + 1) * 256)
+        writes.append(pltpu.make_async_copy(fgrad.at[:, cols], fgrad_h.at[:, cols], done_s.at[1 + p]))
+        writes[-1].start()
     reduce_b()
-    backward_pair(3)
     reduce_y()
 
     for k in range(1, N):
@@ -410,12 +436,28 @@
     for copies in (w_right, w_left, w_side):
         for copy in copies.values():
             copy.wait_send()
+    for write in writes:
+        write.wait()
+
+
+def deliver(out, fgrad, pgrad, out_to, fgrad_to, pgrad_to):
+    out_to[...] = out[...]
+    fgrad_to[...] = fgrad[...]
+    pgrad_to[...] = pgrad[...]
 
 
 def per_device(frames, lengths, taps, conv_bias, norm_gain, proj_weight, cotangent):
-    vmem = pl.BlockSpec(memory_space=pltpu.VMEM)
     dma = pltpu.SemaphoreType.DMA
+    hbm = pl.BlockSpec(memory_space=pltpu.HBM)
+    shapes = (
+        jax.ShapeDtypeStruct((ROWS, D), BF16),
+        jax.ShapeDtypeStruct((ROWS, D), BF16),
+        jax.ShapeDtypeStruct((8, LANES), F32),
+    )
     scratch = [
+        pltpu.VMEM((ROWS, D), BF16), pltpu.VMEM((ROWS, D), BF16), pltpu.VMEM((8, LANES), F32),
+        pltpu.VMEM((ROWS, D), BF16), pltpu.VMEM((N, LANES), jnp.int32), pltpu.VMEM((TAPS, LANES), BF16),
+        pltpu.VMEM((1, LANES), BF16), pltpu.VMEM((1, LANES), BF16), pltpu.VMEM((ROWS, D), BF16),
         pltpu.VMEM((32, LANES), BF16), pltpu.VMEM((16, LANES), BF16), pltpu.VMEM((32, LANES), F32),
         pltpu.VMEM((N, 32, LANES), BF16), pltpu.VMEM((N, 16, LANES), BF16),
         pltpu.VMEM((N, 32, LANES), F32), pltpu.VMEM((N, 16, LANES), F32),
@@ -433,24 +475,28 @@
         pltpu.VMEM((N, 64, LANES), BF16), pltpu.VMEM((N - 1, 64, LANES), BF16),
         pltpu.VMEM((N, 8, LANES), F32), pltpu.VMEM((N - 1, 8, LANES), F32),
         dma((7,)), dma((7,)), dma((7,)), dma((7,)), dma((2,)), dma((2,)), dma((2,)), dma((2,)),
-        dma, dma, dma, dma, dma((4,)), dma((4,)), dma((3,)), dma((3,)), dma((7,)), dma((7,)),
-        dma((7,)), dma((7,)), dma((7,)), dma((7,)), dma((7,)), dma((7,)), dma,
+        dma, dma, dma, dma, dma((4,)), dma((4,)), dma((4,)), dma((4,)), dma((7,)), dma((7,)),
+        dma((7,)), dma((7,)), dma((7,)), dma((7,)), dma((7,)), dma((7,)), dma((7,)), dma((6,)),
     ]
-    return pl.pallas_call(
+    results = pl.pallas_call(
         fused,
-        out_shape=(
-            jax.ShapeDtypeStruct((ROWS, D), BF16),
-            jax.ShapeDtypeStruct((ROWS, D), BF16),
-            jax.ShapeDtypeStruct((8, LANES), F32),
-        ),
-        in_specs=[vmem] * 7,
-        out_specs=(vmem, vmem, vmem),
+        out_shape=shapes,
+        in_specs=[hbm] * 7,
+        out_specs=(hbm,) * 3,
         scratch_shapes=scratch,
         compiler_params=pltpu.CompilerParams(
-            collective_id=0, has_side_effects=True, vmem_limit_bytes=40 * 1024 * 1024),
+            collective_id=0, has_side_effects=True, vmem_limit_bytes=56 * 1024 * 1024),
         name="fused_module",
     )(frames, lengths.reshape(N, LANES), taps, conv_bias.reshape(1, LANES),
       norm_gain.reshape(1, LANES), proj_weight, cotangent)
+    vmem = pl.BlockSpec(memory_space=pltpu.VMEM)
+    return pl.pallas_call(
+        deliver,
+        out_shape=shapes,
+        in_specs=[vmem] * 3,
+        out_specs=(vmem,) * 3,
+        name="deliver",
+    )(*results)
 
 
 def solution(mesh):

time: 70 us -> 63.1 us (0.901)
  local copies, waits for them, and re-layouts: 6.58 us -> 0 us
    unnamed x17 -> x0, local copies, waits for them, and re-layouts: 6.58 us -> none
    pallas_call x1 -> x2, Pallas kernels: 62.4 us -> 62.3 us  [the longest x1 60.1 us: per_device(): pl.pallas_call(fused, out_shape=shapes, in_specs=[hbm] * 7, out_specs=(hb...]
where the time goes in v2:
time: 63.1 us; the launch traced here: 62.9 us
  Pallas kernels  62.3 us (99%)
  between operations  0.64 us (1%)
    pallas_call x1, Pallas kernels, per_device(): pl.pallas_call(fused, out_shape=shapes, in_specs=[hbm] * 7, out_specs=(hb...  60.1 us
    pallas_call x1, Pallas kernels, per_device(): pl.pallas_call(deliver, out_shape=shapes, in_specs=[vmem] * 3, out_specs=...  2.2 us

profile of v2, /device:TPU:1, one launch (start us, length us, event | category | flops | bytes accessed | tf_op | source)
XLA Modules:
  0.0 62.9 jit_solution(16903268757977900188)
XLA Ops:
  0.6 60.1 %fused_module.1 = (bf16[256,1024]{1,0:T(8,128)(2,1)}, bf16[256,1024]{1,0:T(8,128)(2,1)}, f32[8,128]{1,0:T(8,128)}) custom-call(bf16[256,1024]{1,0:T(8,128)(2,1)} %frames_h.1, s32[8,128]{1,0:T(8,128)} %bitcast.3, bf16[31,128]{1,0:T(8,128)(2,1)} %taps_h.1, bf16[1,128]{1,0:T(2,128)(2,1)} %bitcast.4, bf16[1,128]{1,0:T(2,128)(2,1)} %bitcast.5, ...), custom_call_target="tpu_custom_call" | custom-call | tf_op jit(solution)/shard_map/fused_module/pallas_call | solution.py:481
  60.7 2.2 %deliver.1 = (bf16[256,1024]{1,0:T(8,128)(2,1)}, bf16[256,1024]{1,0:T(8,128)(2,1)}, f32[8,128]{1,0:T(8,128)}) custom-call(bf16[256,1024]{1,0:T(8,128)(2,1)} %get-tuple-element.6.out, bf16[256,1024]{1,0:T(8,128)(2,1)} %get-tuple-element.7.fgrad, f32[8,128]{1,0:T(8,128)} %get-tuple-element.8.pgrad), custom_call_target="tpu_custom_call" | custom-call | tf_op jit(solution)/shard_map/deliver/pallas_call | solution.py:493

commit v3 on v2

--- a/solution.py
+++ b/solution.py
@@ -19,8 +19,8 @@
 
 
 def fused(frames_h, lengths_h, taps_h, bias_h, gain_h, weight, cot_h,
-          out_h, fgrad_h, pgrad_h,
-          out, fgrad, pgrad, frames, lengths, taps, bias, gain, cot,
+          out, fgrad, pgrad,
+          frames, lengths, taps, bias, gain, cot,
           pack, gpack, pack_f, tap_all, gain_all, tap_f, gain_f,
           halo, fwin, gwin, off_b, rem_b,
           conv, normed, dfac, inv_b, sum_a, sum_b,
@@ -28,7 +28,7 @@
           tx1, rx1, acc2, tx2, rx2, tx3, rx3,
           tap_s, tap_r, gain_s, gain_r, halo_s, halo_r, ghalo_s, ghalo_r,
           cot_s, cot_r, swt_s, swt_r, wr_s, wr_r, wl_s, wl_r, ws_s, ws_r,
-          r1_s, r1_r, r2_s, r2_r, r3_s, r3_r, loc_s, done_s):
+          r1_s, r1_r, r2_s, r2_r, r3_s, r3_r, loc_s):
     dp = lax.axis_index("dp")
     y = lax.axis_index("fsdp")
     core = dp % 2
@@ -305,6 +305,7 @@
 
     swt_copy = remote(swt.at[1 - core], swt_rx, swt_s, swt_r, sibling)
     swt_copy.start()
+    w_service(2)
     loads[5].wait()
     cot_copy.wait_recv()
     swt_copy.wait_recv()
@@ -320,7 +321,6 @@
         r1[k] = remote(tx1.at[(a + k) % N], rx1.at[k - 1], r1_s.at[k - 1], r1_r.at[k - 1], a_peer(k))
         r1[k].start()
 
-    w_service(2)
     w_service(3)
     w_service(4)
     own_w.wait()
@@ -364,8 +364,6 @@
     for n in range(4):
         cols = slice(n * 256, (n + 1) * 256)
         out[:, cols] = jnp.dot(swished[...], w_all[:, cols], preferred_element_type=F32).astype(BF16)
-    writes = [pltpu.make_async_copy(out, out_h, done_s.at[0])]
-    writes[0].start()
 
     def backward_pair(p, first, count, stride):
         def body(group, carry):
@@ -409,8 +407,6 @@
         for k in range(1, N):
             total = total + rx3[k - 1]
         pgrad[...] = total * (1.0 / 1024)
-        writes.append(pltpu.make_async_copy(pgrad, pgrad_h, done_s.at[5]))
-        writes[-1].start()
 
     for p in range(4):
         backward_pair(p, GROUP, 2, GROUP)
@@ -419,9 +415,6 @@
     ghalo_up.wait_recv()
     for p in range(4):
         backward_pair(p, 0, 2, ROWS - GROUP)
-        cols = slice(p * 256, (p + 1) * 256)
-        writes.append(pltpu.make_async_copy(fgrad.at[:, cols], fgrad_h.at[:, cols], done_s.at[1 + p]))
-        writes[-1].start()
     reduce_b()
     reduce_y()
 
@@ -436,18 +429,20 @@
     for copies in (w_right, w_left, w_side):
         for copy in copies.values():
             copy.wait_send()
-    for write in writes:
-        write.wait()
-
-
-def deliver(out, fgrad, pgrad, out_to, fgrad_to, pgrad_to):
-    out_to[...] = out[...]
-    fgrad_to[...] = fgrad[...]
-    pgrad_to[...] = pgrad[...]
+
+
+def deliver(out, fgrad, pgrad, out_to, fgrad_to, pgrad_to, sem):
+    copies = [pltpu.make_async_copy(src, dst, sem.at[i]) for i, (src, dst) in enumerate(
+        ((out, out_to), (fgrad, fgrad_to), (pgrad, pgrad_to)))]
+    for copy in copies:
+        copy.start()
+    for copy in copies:
+        copy.wait()
 
 
 def per_device(frames, lengths, taps, conv_bias, norm_gain, proj_weight, cotangent):
     dma = pltpu.SemaphoreType.DMA
+    vmem = pl.BlockSpec(memory_space=pltpu.VMEM)
     hbm = pl.BlockSpec(memory_space=pltpu.HBM)
     shapes = (
         jax.ShapeDtypeStruct((ROWS, D), BF16),
@@ -455,7 +450,6 @@
         jax.ShapeDtypeStruct((8, LANES), F32),
     )
     scratch = [
-        pltpu.VMEM((ROWS, D), BF16), pltpu.VMEM((ROWS, D), BF16), pltpu.VMEM((8, LANES), F32),
         pltpu.VMEM((ROWS, D), BF16), pltpu.VMEM((N, LANES), jnp.int32), pltpu.VMEM((TAPS, LANES), BF16),
         pltpu.VMEM((1, LANES), BF16), pltpu.VMEM((1, LANES), BF16), pltpu.VMEM((ROWS, D), BF16),
         pltpu.VMEM((32, LANES), BF16), pltpu.VMEM((16, LANES), BF16), pltpu.VMEM((32, LANES), F32),
@@ -476,27 +470,28 @@
         pltpu.VMEM((N, 8, LANES), F32), pltpu.VMEM((N - 1, 8, LANES), F32),
         dma((7,)), dma((7,)), dma((7,)), dma((7,)), dma((2,)), dma((2,)), dma((2,)), dma((2,)),
         dma, dma, dma, dma, dma((4,)), dma((4,)), dma((4,)), dma((4,)), dma((7,)), dma((7,)),
-        dma((7,)), dma((7,)), dma((7,)), dma((7,)), dma((7,)), dma((7,)), dma((7,)), dma((6,)),
+        dma((7,)), dma((7,)), dma((7,)), dma((7,)), dma((7,)), dma((7,)), dma((7,)),
     ]
     results = pl.pallas_call(
         fused,
         out_shape=shapes,
         in_specs=[hbm] * 7,
-        out_specs=(hbm,) * 3,
+        out_specs=(vmem,) * 3,
         scratch_shapes=scratch,
         compiler_params=pltpu.CompilerParams(
-            collective_id=0, has_side_effects=True, vmem_limit_bytes=56 * 1024 * 1024),
+            collective_id=0, has_side_effects=True, vmem_limit_bytes=40 * 1024 * 1024),
         name="fused_module",
-    )(frames, lengths.reshape(N, LANES), taps, conv_bias.reshape(1, LANES),
-      norm_gain.reshape(1, LANES), proj_weight, cotangent)
-    vmem = pl.BlockSpec(memory_space=pltpu.VMEM)
+    )(*(pltpu.with_memory_space_constraint(value, pltpu.HBM) for value in (
+        frames, lengths.reshape(N, LANES), taps, conv_bias.reshape(1, LANES),
+        norm_gain.reshape(1, LANES), proj_weight, cotangent)))
     return pl.pallas_call(
         deliver,
         out_shape=shapes,
         in_specs=[vmem] * 3,
-        out_specs=(vmem,) * 3,
+        out_specs=(hbm,) * 3,
+        scratch_shapes=[dma((3,))],
         name="deliver",
-    )(*results)
+    )(*(pltpu.with_memory_space_constraint(value, pltpu.VMEM) for value in results))
 
 
 def solution(mesh):

time: 63.1 us -> 60.6 us (0.960)
  Pallas kernels: 62.3 us -> 59.8 us
    pallas_call x1, Pallas kernels: 60.1 us -> 58.8 us  [per_device(): pl.pallas_call(fused, out_shape=shapes, in_specs=[hbm] * 7, out_specs=(vm...]
    pallas_call x1, Pallas kernels: 2.2 us -> 1 us  [per_device(): pl.pallas_call(deliver, out_shape=shapes, in_specs=[vmem] * 3, out_specs=...]
where the time goes in v3:
time: 60.6 us; the launch traced here: 60.4 us
  Pallas kernels  59.8 us (99%)
  between operations  0.64 us (1%)
    pallas_call x1, Pallas kernels, per_device(): pl.pallas_call(fused, out_shape=shapes, in_specs=[hbm] * 7, out_specs=(vm...  58.8 us

profile of v3, /device:TPU:1, one launch (start us, length us, event | category | flops | bytes accessed | tf_op | source)
XLA Modules:
  0.0 60.4 jit_solution(6745228271335628736)
XLA Ops:
  0.6 58.8 %fused_module.1 = (bf16[256,1024]{1,0:T(8,128)(2,1)S(1)}, bf16[256,1024]{1,0:T(8,128)(2,1)S(1)}, f32[8,128]{1,0:T(8,128)S(1)}) custom-call(bf16[256,1024]{1,0:T(8,128)(2,1)} %frames_h.1, s32[8,128]{1,0:T(8,128)} %bitcast.3, bf16[31,128]{1,0:T(8,128)(2,1)} %taps_h.1, bf16[1,128]{1,0:T(2,128)(2,1)} %bitcast.4, bf16[1,128]{1,0:T(2,128)(2,1)} %bitcast.5, ...), custom_call_target="tpu_custom_call" | custom-call | tf_op jit(solution)/shard_map/fused_module/pallas_call | solution.py:475
  59.4 1.0 %deliver.1 = (bf16[256,1024]{1,0:T(8,128)(2,1)}, bf16[256,1024]{1,0:T(8,128)(2,1)}, f32[8,128]{1,0:T(8,128)}) custom-call(bf16[256,1024]{1,0:T(8,128)(2,1)S(1)} %get-tuple-element.6.out, bf16[256,1024]{1,0:T(8,128)(2,1)S(1)} %get-tuple-element.7.fgrad, f32[8,128]{1,0:T(8,128)S(1)} %get-tuple-element.8.pgrad), custom_call_target="tpu_custom_call" | custom-call | tf_op jit(solution)/shard_map/deliver/pallas_call | solution.py:487

commit v4 on v3

--- a/solution.py
+++ b/solution.py
@@ -16,6 +16,7 @@
 HALO = 16
 WIN = ROWS + 2 * HALO
 GROUP = 64
+EARLY = 16
 
 
 def fused(frames_h, lengths_h, taps_h, bias_h, gain_h, weight, cot_h,
@@ -25,10 +26,10 @@
           halo, fwin, gwin, off_b, rem_b,
           conv, normed, dfac, inv_b, sum_a, sum_b,
           swished, swt, swt_f, swt_rx, cot_sib, w_all,
-          tx1, rx1, acc2, tx2, rx2, tx3, rx3,
+          tx1, rx1, acc2, tx2, rx2, tx3, rx3, rxy, txa, rxa, txb, rxb,
           tap_s, tap_r, gain_s, gain_r, halo_s, halo_r, ghalo_s, ghalo_r,
           cot_s, cot_r, swt_s, swt_r, wr_s, wr_r, wl_s, wl_r, ws_s, ws_r,
-          r1_s, r1_r, r2_s, r2_r, r3_s, r3_r, loc_s):
+          r1_s, r1_r, r2_s, r2_r, r3_s, r3_r, ry_s, ry_r, ra_s, ra_r, rb_s, rb_r, loc_s):
     dp = lax.axis_index("dp")
     y = lax.axis_index("fsdp")
     core = dp % 2
@@ -318,10 +319,14 @@
 
     r1 = {}
     for k in order:
-        r1[k] = remote(tx1.at[(a + k) % N], rx1.at[k - 1], r1_s.at[k - 1], r1_r.at[k - 1], a_peer(k))
+        r1[k] = remote(tx1.at[(a + k) % N, EARLY:64], rx1.at[k - 1], r1_s.at[k - 1], r1_r.at[k - 1], a_peer(k))
         r1[k].start()
-
     w_service(3)
+    ry = {}
+    for k in order:
+        ry[k] = remote(tx1.at[:, 0:EARLY, shard((y + k) % N)], rxy.at[k - 1], ry_s.at[k - 1], ry_r.at[k - 1],
+                       y_peer(k))
+        ry[k].start()
     w_service(4)
     own_w.wait()
     for s in range(1, 5):
@@ -361,9 +366,6 @@
     ghalo_down.start()
     ghalo_up.start()
 
-    for n in range(4):
-        cols = slice(n * 256, (n + 1) * 256)
-        out[:, cols] = jnp.dot(swished[...], w_all[:, cols], preferred_element_type=F32).astype(BF16)
 
     def backward_pair(p, first, count, stride):
         def body(group, carry):
@@ -376,54 +378,112 @@
 
         lax.fori_loop(0, count, body, 0)
 
+    late = b >= 2
+
     def reduce_a():
         for k in range(1, N):
-            remote(tx1.at[0], rx1.at[k - 1], r1_s.at[k - 1], r1_r.at[k - 1], a_peer(N - k)).wait_recv()
+            remote(tx1.at[0, EARLY:64], rx1.at[k - 1], r1_s.at[k - 1], r1_r.at[k - 1], a_peer(N - k)).wait_recv()
         for c in range(N):
             cols = slice(c * LANES, (c + 1) * LANES)
-            total = tx1[a, :, cols].astype(F32)
+            total = tx1[a, EARLY:64, cols].astype(F32)
             for k in range(1, N):
                 total = total + rx1[k - 1, :, cols].astype(F32)
-            acc2[:, c] = total.reshape(N, 8, LANES)
-        for i in range(N):
+            acc2[2:N, c] = total.reshape(N - 2, 8, LANES)
+        for i in range(2, N):
             tx2[i] = acc2[i].reshape(64, LANES).astype(BF16)
         for k in order:
-            remote(tx2.at[(b + k) % N], rx2.at[k - 1], r2_s.at[k - 1], r2_r.at[k - 1], b_peer(k)).start()
+            @pl.when((b + k) % N >= 2)
+            def _():
+                remote(tx2.at[(b + k) % N], rx2.at[k - 1], r2_s.at[k - 1], r2_r.at[k - 1], b_peer(k)).start()
+
+    def early_y():
+        for k in range(1, N):
+            remote(rxy.at[k - 1], rxy.at[k - 1], ry_s.at[k - 1], ry_r.at[k - 1], y_peer(N - k)).wait_recv()
+        total = tx1[:, 0:EARLY, shard(y)].astype(F32)
+        for k in range(1, N):
+            total = total + rxy[k - 1].astype(F32)
+        txa[...] = total
+        for k in order:
+            remote(txa.at[(a + k) % N], rxa.at[k - 1], ra_s.at[k - 1], ra_r.at[k - 1], a_peer(k)).start()
+
+    def early_a():
+        for k in range(1, N):
+            remote(txa.at[0], rxa.at[k - 1], ra_s.at[k - 1], ra_r.at[k - 1], a_peer(N - k)).wait_recv()
+        total = txa[a]
+        for k in range(1, N):
+            total = total + rxa[k - 1]
+        txb[...] = total.reshape(2, 8, LANES)
+        for k in order:
+            @pl.when((b + k) % N < 2)
+            def _():
+                remote(txb.at[(b + k) % N % 2], rxb.at[k - 1], rb_s.at[k - 1], rb_r.at[k - 1], b_peer(k)).start()
 
     def reduce_b():
-        for k in range(1, N):
-            remote(tx2.at[0], rx2.at[k - 1], r2_s.at[k - 1], r2_r.at[k - 1], b_peer(N - k)).wait_recv()
-        total = acc2[b].reshape(64, LANES)
-        for k in range(1, N):
-            total = total + rx2[k - 1].astype(F32)
-        tx3[...] = total.reshape(N, 8, LANES)
-        for k in order:
-            remote(tx3.at[(y + k) % N], rx3.at[k - 1], r3_s.at[k - 1], r3_r.at[k - 1], y_peer(k)).start()
-
-    def reduce_y():
-        for k in range(1, N):
-            remote(tx3.at[0], rx3.at[k - 1], r3_s.at[k - 1], r3_r.at[k - 1], y_peer(N - k)).wait_recv()
-        total = tx3[y]
-        for k in range(1, N):
-            total = total + rx3[k - 1]
-        pgrad[...] = total * (1.0 / 1024)
-
+        @pl.when(late)
+        def _():
+            for k in range(1, N):
+                remote(tx2.at[0], rx2.at[k - 1], r2_s.at[k - 1], r2_r.at[k - 1], b_peer(N - k)).wait_recv()
+            total = acc2[b].reshape(64, LANES)
+            for k in range(1, N):
+                total = total + rx2[k - 1].astype(F32)
+            tx3[...] = total.reshape(N, 8, LANES)
+            for k in order:
+                remote(tx3.at[(y + k) % N], rx3.at[k - 1], r3_s.at[k - 1], r3_r.at[k - 1], y_peer(k)).start()
+
+    def finish():
+        @pl.when(late)
+        def _():
+            for k in range(1, N):
+                remote(tx3.at[0], rx3.at[k - 1], r3_s.at[k - 1], r3_r.at[k - 1], y_peer(N - k)).wait_recv()
+            total = tx3[y]
+            for k in range(1, N):
+                total = total + rx3[k - 1]
+            pgrad[...] = total * (1.0 / 1024)
+
+        @pl.when(jnp.logical_not(late))
+        def _():
+            for k in range(1, N):
+                remote(txb.at[0], rxb.at[k - 1], rb_s.at[k - 1], rb_r.at[k - 1], b_peer(N - k)).wait_recv()
+            total = txb[b % 2]
+            for k in range(1, N):
+                total = total + rxb[k - 1]
+            pgrad[...] = total * (1.0 / 1024)
+
+    reduce_a()
+    early_y()
     for p in range(4):
         backward_pair(p, GROUP, 2, GROUP)
-    reduce_a()
     ghalo_down.wait_recv()
     ghalo_up.wait_recv()
-    for p in range(4):
-        backward_pair(p, 0, 2, ROWS - GROUP)
+    backward_pair(0, 0, 2, ROWS - GROUP)
+    backward_pair(1, 0, 2, ROWS - GROUP)
     reduce_b()
-    reduce_y()
+    early_a()
+    backward_pair(2, 0, 2, ROWS - GROUP)
+    backward_pair(3, 0, 2, ROWS - GROUP)
+    for n in range(4):
+        cols = slice(n * 256, (n + 1) * 256)
+        out[:, cols] = jnp.dot(swished[...], w_all[:, cols], preferred_element_type=F32).astype(BF16)
+    finish()
 
     for k in range(1, N):
         tap_copies[k].wait_send()
         gain_copies[k].wait_send()
         r1[k].wait_send()
-        remote(tx2.at[0], rx2.at[k - 1], r2_s.at[k - 1], r2_r.at[k - 1], b_peer(k)).wait_send()
-        remote(tx3.at[0], rx3.at[k - 1], r3_s.at[k - 1], r3_r.at[k - 1], y_peer(k)).wait_send()
+        ry[k].wait_send()
+        remote(txa.at[0], rxa.at[k - 1], ra_s.at[k - 1], ra_r.at[k - 1], a_peer(k)).wait_send()
+
+        @pl.when((b + k) % N >= 2)
+        def _():
+            remote(tx2.at[0], rx2.at[k - 1], r2_s.at[k - 1], r2_r.at[k - 1], b_peer(k)).wait_send()
+
+        @pl.when((b + k) % N < 2)
+        def _():
+            remote(txb.at[0], rxb.at[k - 1], rb_s.at[k - 1], rb_r.at[k - 1], b_peer(k)).wait_send()
+
+        @pl.when(late)
+        def _():
+            remote(tx3.at[0], rx3.at[k - 1], r3_s.at[k - 1], r3_r.at[k - 1], y_peer(k)).wait_send()
     for copy in (halo_down, halo_up, ghalo_down, ghalo_up, cot_copy, swt_copy):
         copy.wait_send()
     for copies in (w_right, w_left, w_side):
@@ -464,12 +524,16 @@
         pltpu.VMEM((ROWS, D), BF16),
         pltpu.VMEM((2, N, 64, ROWS), BF16), pltpu.VMEM((N, N, 8, ROWS), F32), pltpu.VMEM((N, 64, ROWS), BF16),
         pltpu.VMEM((ROWS, D), BF16), pltpu.VMEM((D, D), BF16),
-        pltpu.VMEM((N, 64, D), BF16), pltpu.VMEM((N - 1, 64, D), BF16),
+        pltpu.VMEM((N, 64, D), BF16), pltpu.VMEM((N - 1, 64 - EARLY, D), BF16),
         pltpu.VMEM((N, N, 8, LANES), F32),
         pltpu.VMEM((N, 64, LANES), BF16), pltpu.VMEM((N - 1, 64, LANES), BF16),
         pltpu.VMEM((N, 8, LANES), F32), pltpu.VMEM((N - 1, 8, LANES), F32),
+        pltpu.VMEM((N - 1, N, EARLY, LANES), BF16),
+        pltpu.VMEM((N, EARLY, LANES), F32), pltpu.VMEM((N - 1, EARLY, LANES), F32),
+        pltpu.VMEM((2, 8, LANES), F32), pltpu.VMEM((N - 1, 8, LANES), F32),
         dma((7,)), dma((7,)), dma((7,)), dma((7,)), dma((2,)), dma((2,)), dma((2,)), dma((2,)),
         dma, dma, dma, dma, dma((4,)), dma((4,)), dma((4,)), dma((4,)), dma((7,)), dma((7,)),
+        dma((7,)), dma((7,)), dma((7,)), dma((7,)), dma((7,)), dma((7,)),
         dma((7,)), dma((7,)), dma((7,)), dma((7,)), dma((7,)), dma((7,)), dma((7,)),
     ]
     results = pl.pallas_call(

time: 60.6 us -> 59.9 us (0.988)
  Pallas kernels: 59.8 us -> 58.6 us
    pallas_call x1, Pallas kernels: 58.8 us -> 57.6 us  [per_device(): pl.pallas_call(fused, out_shape=shapes, in_specs=[hbm] * 7, out_specs=(vm...]
where the time goes in v4:
time: 59.9 us; the launch traced here: 59.2 us
  Pallas kernels  58.6 us (98%)
  between operations  0.64 us (1%)
    pallas_call x1, Pallas kernels, per_device(): pl.pallas_call(fused, out_shape=shapes, in_specs=[hbm] * 7, out_specs=(vm...  57.6 us

profile of v4, /device:TPU:1, one launch (start us, length us, event | category | flops | bytes accessed | tf_op | source)
XLA Modules:
  0.0 59.2 jit_solution(12030570503278785672)
XLA Ops:
  0.6 57.6 %fused_module.1 = (bf16[256,1024]{1,0:T(8,128)(2,1)S(1)}, bf16[256,1024]{1,0:T(8,128)(2,1)S(1)}, f32[8,128]{1,0:T(8,128)S(1)}) custom-call(bf16[256,1024]{1,0:T(8,128)(2,1)} %frames_h.1, s32[8,128]{1,0:T(8,128)} %bitcast.3, bf16[31,128]{1,0:T(8,128)(2,1)} %taps_h.1, bf16[1,128]{1,0:T(2,128)(2,1)} %bitcast.4, bf16[1,128]{1,0:T(2,128)(2,1)} %bitcast.5, ...), custom_call_target="tpu_custom_call" | custom-call | tf_op jit(solution)/shard_map/fused_module/pallas_call | solution.py:539
  58.2 1.0 %deliver.1 = (bf16[256,1024]{1,0:T(8,128)(2,1)}, bf16[256,1024]{1,0:T(8,128)(2,1)}, f32[8,128]{1,0:T(8,128)}) custom-call(bf16[256,1024]{1,0:T(8,128)(2,1)S(1)} %get-tuple-element.6.out, bf16[256,1024]{1,0:T(8,128)(2,1)S(1)} %get-tuple-element.7.fgrad, f32[8,128]{1,0:T(8,128)S(1)} %get-tuple-element.8.pgrad), custom_call_target="tpu_custom_call" | custom-call | tf_op jit(solution)/shard_map/deliver/pallas_call | solution.py:551

commit v5 on v4

--- a/solution.py
+++ b/solution.py
@@ -25,7 +25,7 @@
           pack, gpack, pack_f, tap_all, gain_all, tap_f, gain_f,
           halo, fwin, gwin, off_b, rem_b,
           conv, normed, dfac, inv_b, sum_a, sum_b,
-          swished, swt, swt_f, swt_rx, cot_sib, w_all,
+          swished, swt, swt_f, swt_rx, part_f, cot_sib, w_all,
           tx1, rx1, acc2, tx2, rx2, tx3, rx3, rxy, txa, rxa, txb, rxb,
           tap_s, tap_r, gain_s, gain_r, halo_s, halo_r, ghalo_s, ghalo_r,
           cot_s, cot_r, swt_s, swt_r, wr_s, wr_r, wl_s, wl_r, ws_s, ws_r,
@@ -306,14 +306,17 @@
 
     swt_copy = remote(swt.at[1 - core], swt_rx, swt_s, swt_r, sibling)
     swt_copy.start()
+    loads[5].wait()
+    for n in range(4):
+        cols = slice(n * 256, (n + 1) * 256)
+        part_f[:, cols] = jnp.dot(swt[core].reshape(512, ROWS), cot[:, cols], preferred_element_type=F32)
     w_service(2)
-    loads[5].wait()
     cot_copy.wait_recv()
     swt_copy.wait_recv()
 
     for n in range(4):
         cols = slice(n * 256, (n + 1) * 256)
-        part = jnp.dot(swt[core].reshape(512, ROWS), cot[:, cols], preferred_element_type=F32)
+        part = part_f[:, cols]
         part = part + jnp.dot(swt_rx[...].reshape(512, ROWS), cot_sib[:, cols], preferred_element_type=F32)
         tx1[:, :, cols] = part.astype(BF16).reshape(N, 64, 256)
 
@@ -522,7 +525,7 @@
         pltpu.VMEM((N, ROWS, LANES), F32),
         pltpu.VMEM((ROWS, LANES), F32), pltpu.VMEM((ROWS, LANES), F32), pltpu.VMEM((ROWS, LANES), F32),
         pltpu.VMEM((ROWS, D), BF16),
-        pltpu.VMEM((2, N, 64, ROWS), BF16), pltpu.VMEM((N, N, 8, ROWS), F32), pltpu.VMEM((N, 64, ROWS), BF16),
+        pltpu.VMEM((2, N, 64, ROWS), BF16), pltpu.VMEM((N, N, 8, ROWS), F32), pltpu.VMEM((N, 64, ROWS), BF16), pltpu.VMEM((512, D), F32),
         pltpu.VMEM((ROWS, D), BF16), pltpu.VMEM((D, D), BF16),
         pltpu.VMEM((N, 64, D), BF16), pltpu.VMEM((N - 1, 64 - EARLY, D), BF16),
         pltpu.VMEM((N, N, 8, LANES), F32),

time: 59.9 us -> 60 us (level)
  no operation moved by 1% of the time
where the time goes in v5:
time: 60 us; the launch traced here: 59.2 us
  Pallas kernels  58.6 us (98%)
  between operations  0.64 us (1%)
    pallas_call x1, Pallas kernels, per_device(): pl.pallas_call(fused, out_shape=shapes, in_specs=[hbm] * 7, out_specs=(vm...  57.6 us

profile of v5, /device:TPU:1, one launch (start us, length us, event | category | flops | bytes accessed | tf_op | source)
XLA Modules:
  0.0 59.2 jit_solution(15856533257889984080)
XLA Ops:
  0.6 57.6 %fused_module.1 = (bf16[256,1024]{1,0:T(8,128)(2,1)S(1)}, bf16[256,1024]{1,0:T(8,128)(2,1)S(1)}, f32[8,128]{1,0:T(8,128)S(1)}) custom-call(bf16[256,1024]{1,0:T(8,128)(2,1)} %frames_h.1, s32[8,128]{1,0:T(8,128)} %bitcast.3, bf16[31,128]{1,0:T(8,128)(2,1)} %taps_h.1, bf16[1,128]{1,0:T(2,128)(2,1)} %bitcast.4, bf16[1,128]{1,0:T(2,128)(2,1)} %bitcast.5, ...), custom_call_target="tpu_custom_call" | custom-call | tf_op jit(solution)/shard_map/fused_module/pallas_call | solution.py:542
  58.2 1.0 %deliver.1 = (bf16[256,1024]{1,0:T(8,128)(2,1)}, bf16[256,1024]{1,0:T(8,128)(2,1)}, f32[8,128]{1,0:T(8,128)}) custom-call(bf16[256,1024]{1,0:T(8,128)(2,1)S(1)} %get-tuple-element.6.out, bf16[256,1024]{1,0:T(8,128)(2,1)S(1)} %get-tuple-element.7.fgrad, f32[8,128]{1,0:T(8,128)S(1)} %get-tuple-element.8.pgrad), custom_call_target="tpu_custom_call" | custom-call | tf_op jit(solution)/shard_map/deliver/pallas_call | solution.py:554
